TPU v7x, 32 devices: a whole 2x2x4 slice. The times are simulated.
32 devices in a mesh: grp: 4 (over y, x), seq: 8 (over z, core).
Axes of the slice: x: 2, y: 2, z: 4, core: 2. Of those that a mesh axis runs over, the one named last changes fastest.
Arguments:
- queries: bfloat16 [4, 1024, 2048], P('grp', 'seq'), may hold values from -6 to 6
- keys: bfloat16 [4, 1024, 512], P('grp', 'seq'), may hold values from -6 to 6
- values: bfloat16 [4, 1024, 512], P('grp', 'seq'), may hold values from -6 to 6
- route_ids: int32 [4, 1024, 8], P('grp', 'seq'), may hold values from 0 to 31, all different within a row; in each aligned block of 128 rows (0 to 127, 128 to 255, ..., all dimensions but the last counted through in order) at most 36 rows name the same one
- route_weights: float32 [4, 1024, 8], P('grp', 'seq'), may hold values from 0.05 to 0.3
- out_weight: bfloat16 [2048, 2048], replicated, may hold values from -1.5909903 to 1.5909903
- norm_gain: float32 [2048], replicated, may hold values from 0.5 to 1.5
- gate_up: bfloat16 [32, 2048, 1536], P(('grp', 'seq')), may hold values from -0.125 to 0.125
- down_weight: bfloat16 [32, 768, 2048], P(('grp', 'seq')), may hold values from -0.21875 to 0.21875
Outputs:
- mixed: bfloat16 [4, 1024, 2048], P('grp', 'seq')
Inputs may be any that keep to these rules, and one draw needn't show every extreme that they name: `route_ids`: each row names 8 different experts; the rows of one device name no expert more than 36 times, and in some devices' rows some expert exactly 36 times.
All inputs are finite; a program needn't handle non-finite values.
Results may differ from a plain program's by a relative error of at most 0.008.
Values may be sent and summed in bfloat16 or wider, within the bound.
A program may use at most 128 MiB of HBM per device.

v0:
```python
import jax
import jax.numpy as jnp
from jax import lax
from jax.sharding import PartitionSpec as P

D = 2048
QUERY_HEADS = 16
KEY_VALUE_HEADS = 4
HEAD_WIDTH = 128
FF = 768
TOP = 8


def normalize_rows(scores):
    highest = jnp.max(scores, axis=-1, keepdims=True)
    raised = jnp.exp(scores - highest)
    return (raised / jnp.sum(raised, axis=-1, keepdims=True)).astype(jnp.bfloat16)


def on_device(
    queries, keys, values, route_ids, route_weights, out_weight, norm_gain, gate_up, down_weight
):
    token_rows = queries.shape[1]
    heads_per_group = QUERY_HEADS // KEY_VALUE_HEADS
    whole_keys, whole_values = (
        lax.all_gather(keys, "seq", axis=1, tiled=True),
        lax.all_gather(values, "seq", axis=1, tiled=True),
    )
    token_length = whole_keys.shape[1]
    first_row = lax.axis_index("seq") * token_rows
    row_index = first_row + jnp.arange(token_rows, dtype=jnp.int32)[:, None]
    col_index = jnp.arange(token_length, dtype=jnp.int32)[None, :]
    allowed = (col_index <= row_index)[None]
    grouped = queries[0].reshape(token_rows, KEY_VALUE_HEADS, heads_per_group, HEAD_WIDTH)
    results = []
    for kv_index in range(KEY_VALUE_HEADS):
        window = slice(kv_index * HEAD_WIDTH, (kv_index + 1) * HEAD_WIDTH)
        scores = jnp.einsum(
            "tgd,kd->gtk",
            grouped[:, kv_index],
            whole_keys[0, :, window],
            preferred_element_type=jnp.float32,
        ) * HEAD_WIDTH ** (-0.5)
        scores = jnp.where(allowed, scores, -jnp.inf)
        weighted = jnp.einsum(
            "gtk,kd->tgd",
            normalize_rows(scores),
            whole_values[0, :, window],
            preferred_element_type=jnp.float32,
        ).astype(jnp.bfloat16)
        results.append(weighted.reshape(token_rows, heads_per_group * HEAD_WIDTH))
    attended = jnp.concatenate(results, axis=1)
    hidden_state = jnp.dot(attended, out_weight, preferred_element_type=jnp.float32)
    power = jnp.mean(hidden_state * hidden_state, axis=-1, keepdims=True)
    normed = (hidden_state * lax.rsqrt(power + 1e-06) * norm_gain).astype(jnp.bfloat16)
    local_count = gate_up.shape[0]
    experts_all = local_count * lax.axis_size(("grp", "seq"))
    capacity = token_rows * TOP * 9 // (8 * experts_all)
    flat_ids = route_ids[0].reshape(-1)
    onehot = (flat_ids[:, None] == jnp.arange(experts_all, dtype=jnp.int32)[None, :]).astype(
        jnp.int32
    )
    slots = jnp.sum((jnp.cumsum(onehot, axis=0) - onehot) * onehot, axis=1)
    target = flat_ids * capacity + slots
    owners = jnp.arange(token_rows * TOP, dtype=jnp.int32) // TOP
    table = jnp.full((experts_all * capacity,), token_rows, jnp.int32).at[target].set(owners)
    padded = jnp.concatenate([normed, jnp.zeros((1, D), jnp.bfloat16)], axis=0)
    outgoing = padded[table].reshape(experts_all, capacity, D)
    arrived = lax.all_to_all(outgoing, ("grp", "seq"), split_axis=0, concat_axis=0, tiled=True)
    sources = arrived.shape[0] // local_count
    expert_arrived = arrived.reshape(sources, local_count, arrived.shape[1], D)
    both = jnp.einsum("nekd,edf->nekf", expert_arrived, gate_up, preferred_element_type=jnp.float32)
    inner = (jax.nn.silu(both[..., :FF]) * both[..., FF:]).astype(jnp.bfloat16)
    result = (
        jnp.einsum("nekf,efd->nekd", inner, down_weight, preferred_element_type=jnp.float32)
        .astype(jnp.bfloat16)
        .reshape(arrived.shape)
    )
    returned = lax.all_to_all(result, ("grp", "seq"), split_axis=0, concat_axis=0, tiled=True)
    picked = returned.reshape(experts_all * capacity, D)[target]
    weighted = picked.astype(jnp.float32) * route_weights[0].reshape(-1)[:, None]
    mixture = jnp.sum(weighted.reshape(token_rows, TOP, D), axis=1)
    return (hidden_state + mixture).astype(jnp.bfloat16)[None]


def solution(mesh):
    placed = (
        P("grp", "seq", None),
        P("grp", "seq", None),
        P("grp", "seq", None),
        P("grp", "seq", None),
        P("grp", "seq", None),
        P(),
        P(),
        P(("grp", "seq"), None, None),
        P(("grp", "seq"), None, None),
    )
    return jax.shard_map(
        on_device, mesh=mesh, in_specs=placed, out_specs=P("grp", "seq", None), check_vma=False
    )
```

profile of v0, /device:TPU:0, one launch (start us, length us, event | category | flops | bytes accessed | tf_op | source)
XLA Modules:
  0.0 386.5 jit_solution(12285699401173213411)
XLA Ops:
  6.5 0.7 all-gather.3.cloned.1.call-update
  7.3 1.8 copy.18
  9.2 0.8 copy.27
  10.1 0.7 broadcast_multiply_fusion
  10.8 2.0 copy.16
  12.9 9.0 %reduce-window.6 = s32[32,8,128]{2,1,0:T(8,128)S(1)} reduce-window(s32[32,8,128]{2,1,0:T(8,128)S(1)} %fusion.46, s32[]{:T(128)} %constant.46.clone.1), window={size=1x1x128 pad=0_0x0_0x127_0}, to_apply=%region_9.10 | reduce-window | flops 4161536 | bytes 262148 | tf_op jit(solution)/shard_map/reduce-window
  22.6 4.3 %scatter_custom_fusion = s32[1152]{0:T(1024)S(1)} fusion(s32[1024]{0:T(1024)S(1)} %bitcast.255, s32[1024]{0:T(1024)S(1)} %add_select_fusion, s32[]{:T(128)} %constant.16.clone.1), kind=kCustom, calls=%fused_computation.95 | custom fusion | bytes 4612 | tf_op jit(solution)/shard_map/scatter | solution.py:66
  27.1 6.8 %all-gather.3.cloned.1.call-done = bf16[1,1024,512]{2,1,0:T(8,128)(2,1)} async-done(((bf16[1,128,512]{2,1,0:T(8,128)(2,1)}), bf16[1,1024,512]{2,1,0:T(8,128)(2,1)}) %all-gather.3.cloned.1.call-update) | async-done | bytes 1048592 | tf_op jit(solution)/shard_map/all_gather | solution.py:26
  33.9 1.8 fusion.81
  35.7 2.4 fusion.80
  38.0 2.4 fusion.79
  40.4 1.8 fusion.78
  42.2 16.8 %all-gather.5.cloned.1.call-done = bf16[1,1024,512]{1,2,0:T(8,128)(2,1)} async-done(((bf16[1,128,512]{1,2,0:T(8,128)(2,1)}), bf16[1,1024,512]{1,2,0:T(8,128)(2,1)}) %all-gather.5.cloned.1.call-update) | async-done | bytes 1048592 | tf_op jit(solution)/shard_map/all_gather | solution.py:27
  59.0 2.1 convolution_convert_fusion.4
  61.1 2.1 convolution_convert_fusion.3
  63.3 2.2 convolution_convert_fusion.2
  65.5 2.8 convolution_convert_fusion.1
  68.3 4.8 %multiply_reduce_fusion = (f32[128]{0:T(128)S(1)}, f32[128,2048]{1,0:T(8,128)S(1)}) fusion(bf16[2048,2048]{1,0:T(8,128)(2,1)} %param.14, bf16[128,512]{0,1:T(8,128)(2,1)} %bitcast.252, bf16[128,512]{0,1:T(8,128)(2,1)S(1)} %bitcast.251, bf16[128,512]{0,1:T(8,128)(2,1)S(1)} %bitcast.250, bf16[128,512]{0,1:T(8,128)(2,1)S(1)} %bitcast.249), kind=kOutput, calls=%fused_computation.39 | convolution fusion | flops 1076363136 | bytes 9961984 | tf_op jit(solution)/shard_map/dot_general | solution.py:53
  73.2 1.0 copy-done.1
  74.1 0.2 multiply_convert_fusion
  74.3 0.8 concatenate.7
  75.1 11.8 %gather_fusion = bf16[1152,2048]{1,0:T(8,128)(2,1)} fusion(bf16[129,2048]{1,0:T(8,128)(2,1)} %concatenate.7, s32[2048]{0:T(1024)S(1)} %pad_clamp_fusion), kind=kCustom, calls=%fused_computation | custom fusion | bytes 9441792 | tf_op jit(solution)/shard_map/gather | solution.py:68
  86.9 7.2 %reshape.135 = bf16[32,36,2048]{2,1,0:T(8,128)(2,1)} reshape(bf16[1152,2048]{1,0:T(8,128)(2,1)} %gather_fusion) | data formatting | bytes 9437184 | tf_op jit(solution)/shard_map/reshape | solution.py:68
  94.1 120.7 %all_to_all.10 = bf16[32,36,2048]{2,1,0:T(8,128)(2,1)S(1)} all-to-all(bf16[32,36,2048]{2,1,0:T(8,128)(2,1)} %reshape.135), channel_id=1, replica_groups=mesh['grp'=4,'seq'=8] {'grp','seq'}, dimensions={0} | all-to-all | bytes 9437184 | tf_op jit(solution)/shard_map/all_to_all | solution.py:69
  214.8 10.8 %fusion.7 = f32[32,1,36,1536]{3,2,0,1:T(8,128)S(1)} fusion(bf16[32,36,2048]{2,1,0:T(8,128)(2,1)S(1)} %all_to_all.10, bf16[1,2048,1536]{2,1,0:T(8,128)(2,1)} %param.16), kind=kOutput, calls=%fused_computation.11 | convolution fusion | flops 7247757312 | bytes 18087936 | tf_op jit(solution)/shard_map/nekd,edf->nekf/dot_general | solution.py:72
  225.6 6.3 %convolution_convert_fusion = bf16[32,36,2048]{2,1,0:T(8,128)(2,1)} fusion(bf16[1,768,2048]{2,1,0:T(8,128)(2,1)S(1)} %copy-done, f32[32,1,36,1536]{3,2,0,1:T(8,128)S(1)} %fusion.7), kind=kOutput, calls=%fused_computation.12 | convolution fusion | flops 3631546368 | bytes 14942208 | tf_op jit(solution)/shard_map/nekf,efd->nekd/dot_general | solution.py:75
  231.9 3.7 all-to-all-start.1
  235.7 117.4 %all-to-all-done.1 = bf16[32,36,2048]{2,1,0:T(8,128)(2,1)} async-done(((bf16[32,36,2048]{2,1,0:T(8,128)(2,1)}), bf16[32,36,2048]{2,1,0:T(8,128)(2,1)}, u32[]{:S(2)}, u32[]{:S(2)}) %all-to-all-start.1) | async-done | bytes 4718624 | tf_op jit(solution)/shard_map/all_to_all | solution.py:79
  353.1 7.2 %reshape.139 = bf16[1152,2048]{1,0:T(8,128)(2,1)} reshape(bf16[32,36,2048]{2,1,0:T(8,128)(2,1)} %all-to-all-done.1) | data formatting | bytes 9437184 | tf_op jit(solution)/shard_map/reshape | solution.py:80
  360.3 11.8 %gather_fusion.1 = bf16[1024,2048]{1,0:T(8,128)(2,1)} fusion(bf16[1152,2048]{1,0:T(8,128)(2,1)} %reshape.139, s32[1024]{0:T(1024)S(1)} %broadcast_clamp_fusion), kind=kCustom, calls=%fused_computation.1 | custom fusion | bytes 8392704 | tf_op jit(solution)/shard_map/gather | solution.py:80
  372.1 6.6 %fusion.4 = f32[128,2048]{1,0:T(8,128)S(1)} fusion(bf16[1024,2048]{1,0:T(8,128)(2,1)} %gather_fusion.1, f32[128,8]{1,0:T(8,128)S(1)} %copy.31), kind=kLoop, calls=%fused_computation.8 | loop fusion | flops 6029312 | bytes 5246976 | tf_op jit(solution)/shard_map/reduce_sum | solution.py:82
  378.7 0.9 fusion.30
  (35 shorter events, 1.2 us)
Async XLA Ops:
  6.5 219.0 %copy-start = (bf16[1,768,2048]{2,1,0:T(8,128)(2,1)S(1)}, bf16[1,768,2048]{2,1,0:T(8,128)(2,1)}, u32[]{:S(2)}) copy-start(bf16[1,768,2048]{2,1,0:T(8,128)(2,1)} %param.17) | copy-start | bytes 9437188
  6.5 27.4 %all-gather.3.cloned.1.call-start = ((), (), s32[]{:S(2)}) async-start(), calls=%async_computation.2 | async-start | bytes 1179648 | tf_op jit(solution)/shard_map/all_gather | solution.py:26
  7.3 51.7 %all-gather.5.cloned.1.call-start = ((), (), s32[]{:S(2)}) async-start(), calls=%async_computation.3 | async-start | bytes 1179648 | tf_op jit(solution)/shard_map/all_gather | solution.py:27
  27.1 34.0 %copy-start.3 = (pred[128,1024]{0,1:T(8,128)(4,1)}, pred[128,1024]{0,1:T(8,128)(4,1)S(1)}, u32[]{:S(2)}) copy-start(pred[128,1024]{0,1:T(8,128)(4,1)S(1)} %iota_compare_fusion) | copy-start | bytes 393220
  68.3 5.8 %copy-start.4 = (f32[2048]{0:T(1024)S(1)}, f32[2048]{0:T(1024)}, u32[]{:S(2)}) copy-start(f32[2048]{0:T(1024)} %param.15) | copy-start | bytes 24580
  73.1 1.0 copy-start.1
  231.9 3.7 copy-start.5
  231.9 121.2 %all-to-all-start.1 = ((bf16[32,36,2048]{2,1,0:T(8,128)(2,1)}), bf16[32,36,2048]{2,1,0:T(8,128)(2,1)}, u32[]{:S(2)}, u32[]{:S(2)}) async-start(bf16[32,36,2048]{2,1,0:T(8,128)(2,1)} %convolution_convert_fusion), calls=%async_computation.1 | async-start | bytes 10485760 | tf_op jit(solution)/shard_map/all_to_all | solution.py:79
  372.1 6.6 %copy-start.2 = (f32[128,2048]{1,0:T(8,128)S(1)}, f32[128,2048]{1,0:T(8,128)}, u32[]{:S(2)}) copy-start(f32[128,2048]{1,0:T(8,128)} %copy-done.1) | copy-start | bytes 3145732
Sparse Core Ops, SparseCore 0:
  9.0 24.8 all-gather.2
  35.5 23.4 all-gather.4
where the time goes:
time: 387 us; the launch traced here: 386 us
  waiting for transfers between devices  142 us (37%)
  blocking collectives  121 us (31%)
  local copies, waits for them, and re-layouts  49.6 us (13%)
  matrix products  39.4 us (10%)
  other arithmetic  17.7 us (5%)
  between operations  13.6 us (4%)
    all_to_all x1, blocking collectives, on_device(): lax.all_to_all(outgoing, ('grp', 'seq'), split_axis=0, concat_axis=0, til...  121 us
    all_to_all x1, waiting for transfers between devices, on_device(): lax.all_to_all(result, ('grp', 'seq'), split_axis=0, concat_axis=0, tiled...  117 us
    all_gather x1, waiting for transfers between devices, on_device(): lax.all_gather(values, 'seq', axis=1, tiled=True)  16.8 us
    gather x1, local copies, waits for them, and re-layouts, on_device(): outgoing = padded[table].reshape(experts_all, capacity, D)  11.8 us
    gather x1, local copies, waits for them, and re-layouts, on_device(): picked = returned.reshape(experts_all * capacity, D)[target]  11.8 us
    dot_general x1, matrix products, on_device(): jnp.einsum('nekd,edf->nekf', expert_arrived, gate_up, preferred_element_t...  10.8 us
    dot_general x4, matrix products, on_device(): jnp.einsum('gtk,kd->tgd', normalize_rows(scores), whole_values[0, :, wind...  9.27 us
    another operation x3, other arithmetic  9.15 us
  transfers between devices with their start and end apart: 3, of which 3 were waited for; matrix products, arithmetic and copies ran while one was open for 7% of the time, Pallas kernels for 0%

commit v1 on v0

v1 whole, which is shorter than its diff:
```python
import functools

import jax
import jax.numpy as jnp
from jax import lax
from jax.experimental import pallas as pl
from jax.experimental.pallas import tpu as pltpu
from jax.sharding import PartitionSpec as P

HEAD_WIDTH = 128
MESH = pl.DeviceIdType.MESH
CORES = 2
CHUNK = 512


def normalize_rows(scores):
    highest = jnp.max(scores, axis=-1, keepdims=True)
    raised = jnp.exp(scores - highest)
    return (raised / jnp.sum(raised, axis=-1, keepdims=True)).astype(jnp.bfloat16)


def loop(low, high, body):
    lax.fori_loop(low, high, lambda i, carry: (body(i), carry)[1], 0)


def expert_kernel(
    line, plane,
    normed, hidden, sel, share, gate_hbm, down_hbm,
    out,
    rows, packed, arrived, both, gate, down, inner, returned, own, part_out, part_in,
    line_s1, line_r1, plane_s1, plane_r1, plane_s2, plane_r2, line_s2, line_r2, load_sem,
):
    tokens = normed.shape[0]
    parts = rows.shape[0]
    slots = sel.shape[0] // plane
    half = gate.shape[1] // 2
    group = lax.axis_index("grp")
    place = lax.axis_index("seq")
    z, core = place // CORES, place % CORES
    me = group * CORES + core

    def on_line(k):
        other = (z + k) % line
        return other, (group, other * CORES + core)

    def on_plane(k):
        other = (me + k) % plane
        return other, (other // CORES, z * CORES + other % CORES)

    def block(i):
        return pl.ds(pl.multiple_of(i * slots, 16), slots)

    def tok(i):
        return pl.ds(pl.multiple_of(i * tokens, 16), tokens)

    def columns(i, width):
        return pl.ds(pl.multiple_of(i * width, 128), width)

    def line1(c, k):
        _, device = on_line(k)
        mine = rows.at[c, tok(z)]
        return pltpu.make_async_remote_copy(
            mine, mine, line_s1.at[c, k - 1], line_r1.at[c, k - 1], device_id=device, device_id_type=MESH
        )

    def plane1(c, k):
        other, device = on_plane(k)
        return pltpu.make_async_remote_copy(
            packed.at[c, block(other)], arrived.at[c, block(me)],
            plane_s1.at[c, k - 1], plane_r1.at[c, k - 1], device_id=device, device_id_type=MESH,
        )

    def plane2(c, k):
        other, device = on_plane(k)
        return pltpu.make_async_remote_copy(
            packed.at[c, block(other)], returned.at[c, block(me)],
            plane_s2.at[c, k - 1], plane_r2.at[c, k - 1], device_id=device, device_id_type=MESH,
        )

    def line2(c, k):
        other, device = on_line(k)
        return pltpu.make_async_remote_copy(
            part_out.at[c, tok(other)], part_in.at[c, k - 1],
            line_s2.at[c, k - 1], line_r2.at[c, k - 1], device_id=device, device_id_type=MESH,
        )

    load_gate = pltpu.make_async_copy(gate_hbm.at[0], gate, load_sem.at[0])
    load_down = pltpu.make_async_copy(down_hbm.at[0], down, load_sem.at[1])
    load_gate.start()
    load_down.start()

    barrier = pltpu.get_barrier_semaphore()
    for k in range(1, line):
        pl.semaphore_signal(barrier, inc=1, device_id=on_line(k)[1], device_id_type=MESH)
    for k in range(1, plane):
        pl.semaphore_signal(barrier, inc=1, device_id=on_plane(k)[1], device_id_type=MESH)
    pl.semaphore_wait(barrier, line + plane - 2)

    for c in range(parts):
        rows[c, tok(z), :] = normed[:, c * CHUNK : (c + 1) * CHUNK]
        loop(1, line, lambda k: line1(c, k).start())

    def picked(c, other):
        return jnp.dot(sel[block(other), :], rows[c], preferred_element_type=jnp.float32).astype(jnp.bfloat16)

    def pack(c):
        loop(1, line, lambda k: line1(c, k).wait_recv())

        def one(k):
            other, _ = on_plane(k)
            packed[c, block(other), :] = picked(c, other)
            plane1(c, k).start()

        loop(1, plane, one)
        arrived[c, block(me), :] = picked(c, me)

    def first(c):
        if c == 0:
            load_gate.wait()
        loop(1, plane, lambda k: plane1(c, k).wait_recv())

        def one(n):
            cols = columns(n, 256)
            term = jnp.dot(
                arrived[c], gate[c * CHUNK : (c + 1) * CHUNK, cols], preferred_element_type=jnp.float32
            )
            if c == 0:
                both[:, cols] = term
            else:
                both[:, cols] += term

        loop(0, 2 * half // 256, one)

    pack(0)
    for c in range(1, parts):
        pack(c)
        first(c - 1)
    first(parts - 1)

    def activate(i):
        g = both[block(i), :half]
        inner[block(i), :] = (g / (1.0 + jnp.exp(-g)) * both[block(i), half:]).astype(jnp.bfloat16)

    loop(0, plane, activate)
    load_down.wait()

    for c in range(parts):
        loop(1, plane, lambda k: plane1(c, k).wait_send())

        def second(n):
            packed[c, :, columns(n, 256)] = jnp.dot(
                inner[...], down[:, columns(n + c * (CHUNK // 256), 256)], preferred_element_type=jnp.float32
            ).astype(jnp.bfloat16)

        loop(0, CHUNK // 256, second)
        loop(1, plane, lambda k: plane2(c, k).start())
        returned[c, block(me), :] = packed[c, block(me), :]

    for c in range(parts):
        loop(1, plane, lambda k: plane2(c, k).wait_recv())

        def summed(other):
            return jnp.dot(share[tok(other), :], returned[c], preferred_element_type=jnp.float32)

        def send(k):
            other, _ = on_line(k)
            part_out[c, tok(other), :] = summed(other).astype(jnp.bfloat16)
            line2(c, k).start()

        loop(1, line, send)
        own[c] = summed(z)

    for c in range(parts):
        loop(1, line, lambda k: line2(c, k).wait_recv())
        total = hidden[:, c * CHUNK : (c + 1) * CHUNK] + own[c]
        for k in range(1, line):
            total += part_in[c, k - 1].astype(jnp.float32)
        out[:, c * CHUNK : (c + 1) * CHUNK] = total.astype(jnp.bfloat16)

    for c in range(parts):
        loop(1, line, lambda k: line1(c, k).wait_send())
        loop(1, plane, lambda k: plane2(c, k).wait_send())
        loop(1, line, lambda k: line2(c, k).wait_send())


def experts(normed, hidden, sel, share, gate_up, down_weight, line, plane):
    tokens, width = normed.shape
    parts = width // CHUNK
    total, gathered = sel.shape
    half = down_weight.shape[1]
    bf16, f32 = jnp.bfloat16, jnp.float32
    vmem = pl.BlockSpec(memory_space=pltpu.VMEM)
    anywhere = pl.BlockSpec(memory_space=pl.ANY)
    dma = pltpu.SemaphoreType.DMA
    on_line, on_plane = dma((parts, line - 1)), dma((parts, plane - 1))
    return pl.pallas_call(
        functools.partial(expert_kernel, line, plane),
        out_shape=jax.ShapeDtypeStruct((tokens, width), bf16),
        in_specs=[vmem, vmem, vmem, vmem, anywhere, anywhere],
        out_specs=vmem,
        scratch_shapes=[
            pltpu.VMEM((parts, gathered, CHUNK), bf16),
            pltpu.VMEM((parts, total, CHUNK), bf16),
            pltpu.VMEM((parts, total, CHUNK), bf16),
            pltpu.VMEM((total, 2 * half), f32),
            pltpu.VMEM((width, 2 * half), bf16),
            pltpu.VMEM((half, width), bf16),
            pltpu.VMEM((total, half), bf16),
            pltpu.VMEM((parts, total, CHUNK), bf16),
            pltpu.VMEM((parts, tokens, CHUNK), f32),
            pltpu.VMEM((parts, gathered, CHUNK), bf16),
            pltpu.VMEM((parts, line - 1, tokens, CHUNK), bf16),
            on_line, on_line, on_plane, on_plane, on_plane, on_plane, on_line, on_line, dma((2,)),
        ],
        compiler_params=pltpu.CompilerParams(
            collective_id=0, has_side_effects=True, vmem_limit_bytes=60 * 2**20
        ),
        cost_estimate=pl.CostEstimate(
            flops=6 * total * width * half, bytes_accessed=6 * width * half, transcendentals=total * half
        ),
    )(normed, hidden, sel, share, gate_up, down_weight)


def routing(route_ids, route_weights, line, plane, experts_all):
    tokens, top = route_ids.shape[1:]
    n_seq = lax.axis_size("seq")
    place = lax.axis_index("seq")
    z, core = place // CORES, place % CORES
    capacity = tokens * top * 9 // (8 * experts_all)
    slots = -(-line * capacity // 16) * 16
    both = jnp.concatenate([route_ids[0].astype(jnp.float32), route_weights[0]], axis=1)
    both = lax.all_gather(both, "seq", axis=0).reshape(line, CORES, tokens, 2 * top)
    both = lax.dynamic_index_in_dim(both, core, 1, keepdims=False)
    ids, weights = both[..., :top].astype(jnp.int32), both[..., top:]
    members = jnp.arange(plane, dtype=jnp.int32)
    here = members // CORES * n_seq + z * CORES + members % CORES
    match = ids[..., None] == here
    named = jnp.any(match, axis=2)
    weight = jnp.sum(jnp.where(match, weights[..., None], 0.0), axis=2)
    order = jnp.arange(tokens)
    before = (order[None, :] < order[:, None]).astype(jnp.bfloat16)
    slot = jnp.einsum("ts,lsp->ltp", before, named.astype(jnp.bfloat16), preferred_element_type=jnp.float32)
    first = jnp.arange(line, dtype=jnp.int32)[:, None, None] * capacity
    target = jnp.where(named, slot.astype(jnp.int32) + first, -1).reshape(line * tokens, plane)
    weight = weight.reshape(line * tokens, plane)
    at = jnp.arange(slots, dtype=jnp.int32)
    sel = (target.T[:, None, :] == at[None, :, None]).astype(jnp.bfloat16)
    share = jnp.where(target[:, :, None] == at, weight[:, :, None], 0.0).astype(jnp.bfloat16)
    return sel.reshape(plane * slots, line * tokens), share.reshape(line * tokens, plane * slots)


def attention(queries, keys, values):
    token_rows = queries.shape[1]
    kv_heads = keys.shape[2] // HEAD_WIDTH
    heads_per_group = queries.shape[2] // keys.shape[2]
    whole_keys, whole_values = (
        lax.all_gather(keys, "seq", axis=1, tiled=True),
        lax.all_gather(values, "seq", axis=1, tiled=True),
    )
    token_length = whole_keys.shape[1]
    first_row = lax.axis_index("seq") * token_rows
    row_index = first_row + jnp.arange(token_rows, dtype=jnp.int32)[:, None]
    col_index = jnp.arange(token_length, dtype=jnp.int32)[None, :]
    allowed = (col_index <= row_index)[None]
    grouped = queries[0].reshape(token_rows, kv_heads, heads_per_group, HEAD_WIDTH)
    results = []
    for kv_index in range(kv_heads):
        window = slice(kv_index * HEAD_WIDTH, (kv_index + 1) * HEAD_WIDTH)
        scores = jnp.einsum(
            "tgd,kd->gtk",
            grouped[:, kv_index],
            whole_keys[0, :, window],
            preferred_element_type=jnp.float32,
        ) * HEAD_WIDTH ** (-0.5)
        scores = jnp.where(allowed, scores, -jnp.inf)
        weighted = jnp.einsum(
            "gtk,kd->tgd",
            normalize_rows(scores),
            whole_values[0, :, window],
            preferred_element_type=jnp.float32,
        ).astype(jnp.bfloat16)
        results.append(weighted.reshape(token_rows, heads_per_group * HEAD_WIDTH))
    return jnp.concatenate(results, axis=1)


def on_device(
    queries, keys, values, route_ids, route_weights, out_weight, norm_gain, gate_up, down_weight
):
    n_grp, n_seq = lax.axis_size("grp"), lax.axis_size("seq")
    line, plane = n_seq // CORES, n_grp * CORES
    sel, share = routing(route_ids, route_weights, line, plane, n_grp * n_seq)
    attended = attention(queries, keys, values)
    hidden_state = jnp.dot(attended, out_weight, preferred_element_type=jnp.float32)
    power = jnp.mean(hidden_state * hidden_state, axis=-1, keepdims=True)
    normed = (hidden_state * lax.rsqrt(power + 1e-06) * norm_gain).astype(jnp.bfloat16)
    return experts(normed, hidden_state, sel, share, gate_up, down_weight, line, plane)[None]


def solution(mesh):
    placed = (
        P("grp", "seq", None),
        P("grp", "seq", None),
        P("grp", "seq", None),
        P("grp", "seq", None),
        P("grp", "seq", None),
        P(),
        P(),
        P(("grp", "seq"), None, None),
        P(("grp", "seq"), None, None),
    )
    return jax.shard_map(
        on_device, mesh=mesh, in_specs=placed, out_specs=P("grp", "seq", None), check_vma=False
    )
```

time: 387 us -> 226 us (0.58)
  Pallas kernels: 0 us -> 143 us
  waiting for transfers between devices: 142 us -> 17.4 us
  blocking collectives: 121 us -> 15.6 us
  local copies, waits for them, and re-layouts: 49.6 us -> 11.2 us
  matrix products: 39.4 us -> 14.5 us
  other arithmetic: 17.7 us -> 6.72 us
    pallas_call x0 -> x1, Pallas kernels: none -> 143 us  [experts(): pl.pallas_call(functools.partial(expert_kernel, line, plane), out_shape=j...]
    all_to_all x1 -> x0, blocking collectives: 121 us -> none  [on_device(): lax.all_to_all(outgoing, ('grp', 'seq'), split_axis=0, concat_axis=0, til...]
    all_to_all x1 -> x0, waiting for transfers between devices: 117 us -> none  [on_device(): lax.all_to_all(result, ('grp', 'seq'), split_axis=0, concat_axis=0, tiled...]
    gather x2 -> x0, local copies, waits for them, and re-layouts: 23.5 us -> none  [the longest x1 11.8 us: on_device(): outgoing = padded[table].reshape(experts_all, capacity, D)]
    dot_general x6 -> x5, matrix products: 26.3 us -> 5.4 us  [the longest x4 5.29 us: attention(): jnp.einsum('gtk,kd->tgd', normalize_rows(scores), whole_values[0, :, wind...]
    all_gather x0 -> x1, blocking collectives: none -> 15.6 us  [routing(): lax.all_gather(both, 'seq', axis=0).reshape(line, CORES, tokens, 2 * top)]
    reshape x2 -> x1, local copies, waits for them, and re-layouts: 14.4 us -> 0.06 us  [routing(): lax.all_gather(both, 'seq', axis=0).reshape(line, CORES, tokens, 2 * top)]
    another operation x3 -> x0, other arithmetic: 9.15 us -> none
  transfers between devices with their start and end apart: 3 -> 2, of which waited for: 3 -> 1; matrix products, arithmetic and copies ran while one was open for 7% -> 9% of each run, Pallas kernels for 0% -> 0%
where the time goes in v1:
time: 226 us; the launch traced here: 223 us
  Pallas kernels  143 us (63%)
  waiting for transfers between devices  17.4 us (8%)
  blocking collectives  15.6 us (7%)
  matrix products  14.5 us (6%)
  between operations  13.6 us (6%)
  local copies, waits for them, and re-layouts  11.2 us (5%)
  other arithmetic  6.72 us (3%)
    pallas_call x1, Pallas kernels, experts(): pl.pallas_call(functools.partial(expert_kernel, line, plane), out_shape=j...  143 us
    all_gather x1, waiting for transfers between devices, attention(): lax.all_gather(values, 'seq', axis=1, tiled=True)  16.7 us
    all_gather x1, blocking collectives, routing(): lax.all_gather(both, 'seq', axis=0).reshape(line, CORES, tokens, 2 * top)  15.6 us
    unnamed x19, local copies, waits for them, and re-layouts  5.72 us
    dot_general x4, matrix products, attention(): jnp.einsum('gtk,kd->tgd', normalize_rows(scores), whole_values[0, :, wind...  5.29 us
    dot_general x1, matrix products, on_device(): jnp.dot(attended, out_weight, preferred_element_type=jnp.float32)  4.74 us
  transfers between devices with their start and end apart: 2, of which 1 were waited for; matrix products, arithmetic and copies ran while one was open for 9% of the time, Pallas kernels for 0%

profile of v1, /device:TPU:0, one launch (start us, length us, event | category | flops | bytes accessed | tf_op | source)
XLA Modules:
  0.0 222.5 jit_solution(17860884351047969622)
XLA Ops:
  6.5 0.7 all-gather.4.cloned.1.call-update
  7.3 0.0 all-gather.6.cloned.1.call-start
  7.3 1.7 copy.47
  9.0 0.7 convert_bitcast_fusion
  9.7 0.7 pad_maximum_fusion
  10.4 15.6 %all-gather = f32[1024,16]{0,1:T(8,128)S(1)} all-gather(f32[128,16]{0,1:T(8,128)S(1)} %pad_maximum_fusion), channel_id=2, replica_groups=mesh['grp'=4,'seq'=8] {'seq'}, dimensions={0}, use_global_device_ids=true | all-gather | bytes 73728 | tf_op jit(solution)/shard_map/all_gather | solution.py:232
  26.0 0.1 reshape.104
  26.2 0.1 compare_reduce_fusion
  26.3 0.1 fusion.11
  26.4 1.8 eq.66
  28.1 2.0 copy.56
  30.2 0.1 fusion.36
  30.3 0.1 broadcast_in_dim.87
  30.4 1.4 copy.57
  31.8 0.1 eq.63
  31.9 2.1 copy.45
  34.0 2.0 fusion.4.sel
  36.0 0.7 iota_compare_fusion
  36.8 1.3 select_convert_fusion.share
  38.1 2.0 fusion.71
  40.1 0.8 fusion.70
  40.9 0.8 fusion.69
  41.7 0.8 fusion.68
  42.4 16.7 %all-gather.6.cloned.1.call-done = bf16[1,1024,512]{1,2,0:T(8,128)(2,1)} async-done(((bf16[1,128,512]{1,2,0:T(8,128)(2,1)}), bf16[1,1024,512]{1,2,0:T(8,128)(2,1)}) %all-gather.6.cloned.1.call-update) | async-done | bytes 1048592 | tf_op jit(solution)/shard_map/all_gather | solution.py:258
  59.2 2.1 convolution_convert_fusion.3
  61.3 1.1 convolution_convert_fusion.2
  62.4 1.1 convolution_convert_fusion.1
  63.4 1.1 convolution_convert_fusion
  64.5 4.7 %multiply_reduce_fusion = (f32[128]{0:T(128)S(1)}, f32[128,2048]{1,0:T(8,128)S(1)}) fusion(bf16[2048,2048]{1,0:T(8,128)(2,1)} %param.14, bf16[128,512]{0,1:T(8,128)(2,1)S(1)} %bitcast.235, bf16[128,512]{0,1:T(8,128)(2,1)S(1)} %bitcast.234, bf16[128,512]{0,1:T(8,128)(2,1)S(1)} %bitcast.233, bf16[128,512]{0,1:T(8,128)(2,1)S(1)} %bitcast.232), kind=kOutput, calls=%fused_computation.32 | convolution fusion | flops 1076363136 | bytes 9961984 | tf_op jit(solution)/shard_map/dot_general | solution.py:293
  69.3 1.1 multiply_convert_fusion.normed
  70.4 143.4 %shard_map.91 = bf16[128,2048]{1,0:T(8,128)(2,1)} custom-call(bf16[128,2048]{1,0:T(8,128)(2,1)} %multiply_convert_fusion.normed, f32[128,2048]{1,0:T(8,128)} %copy-done.1, bf16[1152,512]{1,0:T(8,128)(2,1)} %fusion.4.sel, bf16[512,1152]{1,0:T(8,128)(2,1)} %select_convert_fusion.share, bf16[1,2048,1536]{2,1,0:T(8,128)(2,1)} %gate_hbm.1, ...), custom_call_target="tpu_custom_call" | custom-call | flops 10871635968 | bytes 9437184 | tf_op jit(solution)/shard_map/pallas_call | solution.py:196
  213.8 1.9 copy.69
  (27 shorter events, 0.1 us)
Async XLA Ops:
  6.5 31.6 %all-gather.4.cloned.1.call-start = ((), (), s32[]{:S(2)}) async-start(), calls=%async_computation | async-start | bytes 1179648 | tf_op jit(solution)/shard_map/all_gather | solution.py:257
  7.3 51.9 %all-gather.6.cloned.1.call-start = ((), (), s32[]{:S(2)}) async-start(), calls=%async_computation.1 | async-start | bytes 1179648 | tf_op jit(solution)/shard_map/all_gather | solution.py:258
  26.4 1.8 copy-start.4
  31.8 5.0 %copy-start = (bf16[512,1152]{1,0:T(8,128)(2,1)S(1)}, bf16[512,1152]{1,0:T(8,128)(2,1)}, u32[]{:S(2)}) copy-start(bf16[512,1152]{1,0:T(8,128)(2,1)} %copy.57) | copy-start | bytes 3538948
  38.1 2.0 copy-start.2
  38.1 2.0 copy-start.3
  38.1 2.0 copy-start.6
  59.2 2.1 copy-start.7
  64.5 4.8 %copy-start.5 = (f32[2048]{0:T(1024)S(1)}, f32[2048]{0:T(1024)}, u32[]{:S(2)}) copy-start(f32[2048]{0:T(1024)} %param.15) | copy-start | bytes 24580
  69.3 1.1 copy-start.1
Sparse Core Ops, SparseCore 0:
  9.0 24.8 all-gather.3
  35.4 23.6 all-gather.5

commit v2 on v1

--- a/solution.py
+++ b/solution.py
@@ -10,13 +10,7 @@
 HEAD_WIDTH = 128
 MESH = pl.DeviceIdType.MESH
 CORES = 2
-CHUNK = 512
-
-
-def normalize_rows(scores):
-    highest = jnp.max(scores, axis=-1, keepdims=True)
-    raised = jnp.exp(scores - highest)
-    return (raised / jnp.sum(raised, axis=-1, keepdims=True)).astype(jnp.bfloat16)
+CHUNK = 256
 
 
 def loop(low, high, body):
@@ -221,66 +215,211 @@
     )(normed, hidden, sel, share, gate_up, down_weight)
 
 
-def routing(route_ids, route_weights, line, plane, experts_all):
-    tokens, top = route_ids.shape[1:]
-    n_seq = lax.axis_size("seq")
+def attention_kernel(
+    line, plane, capacity,
+    queries, keys, values, ids, weights, gain, weight_hbm,
+    hidden, normed, sel, share,
+    kv, route, attended, weight, kv_s1, kv_r1, kv_s2, kv_r2, mate_sem, route_s, route_r, load_sem,
+):
+    tokens, width = queries.shape
+    kv_width = keys.shape[1]
+    everything = kv.shape[0]
+    padded = route.shape[2] // 2
+    slots = sel.shape[0] // plane
+    bf16, f32 = jnp.bfloat16, jnp.float32
+    group = lax.axis_index("grp")
     place = lax.axis_index("seq")
     z, core = place // CORES, place % CORES
-    capacity = tokens * top * 9 // (8 * experts_all)
+    mate = (group, z * CORES + 1 - core)
+
+    def tok(i):
+        return pl.ds(pl.multiple_of(i * tokens, 16), tokens)
+
+    def to(k):
+        return group, ((z + k) % line) * CORES + core
+
+    def line_kv(k):
+        mine = kv.at[tok(place)]
+        return pltpu.make_async_remote_copy(
+            mine, mine, kv_s1.at[k - 1], kv_r1.at[k - 1], device_id=to(k), device_id_type=MESH
+        )
+
+    def mate_kv(k):
+        held = kv.at[tok((z - k) * CORES + core)]
+        return pltpu.make_async_remote_copy(
+            held, held, kv_s2.at[k - 1], kv_r2.at[k - 1], device_id=mate, device_id_type=MESH
+        )
+
+    def own_kv():
+        mine = kv.at[tok(place)]
+        return pltpu.make_async_remote_copy(
+            mine, mine, mate_sem.at[0], mate_sem.at[1], device_id=mate, device_id_type=MESH
+        )
+
+    def line_route(k):
+        mine = route.at[z]
+        return pltpu.make_async_remote_copy(
+            mine, mine, route_s.at[k - 1], route_r.at[k - 1], device_id=to(k), device_id_type=MESH
+        )
+
+    load = pltpu.make_async_copy(weight_hbm, weight, load_sem)
+    load.start()
+
+    barrier = pltpu.get_barrier_semaphore()
+    for k in range(1, line):
+        pl.semaphore_signal(barrier, inc=1, device_id=to(k), device_id_type=MESH)
+    pl.semaphore_signal(barrier, inc=1, device_id=mate, device_id_type=MESH)
+    pl.semaphore_wait(barrier, line)
+
+    kv[tok(place), :kv_width] = keys[...]
+    kv[tok(place), kv_width:] = values[...]
+    loop(1, line - z, lambda k: line_kv(k).start())
+
+    @pl.when(core == 0)
+    def _():
+        own_kv().start()
+
+    lanes = lax.broadcasted_iota(jnp.int32, (tokens, padded), 1)
+    shares = jnp.zeros((tokens, padded), f32)
+    named = jnp.zeros((tokens, padded), f32)
+    for j in range(ids.shape[1]):
+        match = lanes == ids[:, j : j + 1]
+        shares = jnp.where(match, weights[:, j : j + 1], shares)
+        named = jnp.where(match, 1.0, named)
+    square = (tokens, tokens)
+    before = lax.broadcasted_iota(jnp.int32, square, 1) < lax.broadcasted_iota(jnp.int32, square, 0)
+    before = jnp.where(before, 1.0, 0.0).astype(bf16)
+    slot = jnp.dot(before, named.astype(bf16), preferred_element_type=f32)
+    route[z, :, :padded] = jnp.where(named > 0.5, slot, -1024.0).astype(bf16)
+    route[z, :, padded:] = shares.astype(bf16)
+    loop(1, line, lambda k: line_route(k).start())
+
+    def clear(i):
+        kv[tok(i), :] = jnp.zeros((tokens, 2 * kv_width), bf16)
+
+    loop(place + 1, everything // tokens, clear)
+
+    n_seq = line * CORES
+    total = plane * slots
+    q = lax.broadcasted_iota(jnp.int32, (1, total), 1)
+    expert, row = q * 0 + z * CORES, q
+    for i in range(1, plane):
+        past = q >= i * slots
+        expert = expert + jnp.where(past, 1 if i % CORES else n_seq - CORES + 1, 0)
+        row = row - jnp.where(past, slots, 0)
+    spread = jnp.where(lax.broadcasted_iota(jnp.int32, (padded, total), 0) == expert, 1.0, 0.0).astype(bf16)
+    row = row.astype(f32)
+    down_rows = lax.broadcasted_iota(jnp.int32, (slots, tokens), 0).astype(f32)
+    pick_lanes = lax.broadcasted_iota(jnp.int32, (slots, padded), 1)
+
+    loop(1, line, lambda k: line_route(k).wait_recv())
+    for l in range(line):
+        at = jnp.dot(route[l, :, :padded], spread, preferred_element_type=f32)
+        part = jnp.dot(route[l, :, padded:], spread, preferred_element_type=f32)
+        share[l * tokens : (l + 1) * tokens, :] = jnp.where(at + l * capacity == row, part, 0.0).astype(bf16)
+
+    def choose(p):
+        pick = p // CORES * n_seq + z * CORES + p % CORES
+        pick = jnp.where(pick_lanes == pick, 1.0, 0.0).astype(bf16)
+        for l in range(line):
+            at = lax.dot_general(
+                pick, route[l, :, :padded], (((1,), (1,)), ((), ())), preferred_element_type=f32
+            )
+            sel[pl.ds(pl.multiple_of(p * slots, 16), slots), l * tokens : (l + 1) * tokens] = jnp.where(
+                at + l * capacity == down_rows, 1.0, 0.0
+            ).astype(bf16)
+
+    loop(0, plane, choose)
+
+    def forward(k):
+        line_kv(k).wait_recv()
+        mate_kv(k).start()
+
+    loop(1, z + 1, forward)
+    loop(1, z + 1, lambda k: mate_kv(k).wait_recv())
+
+    @pl.when(core == 1)
+    def _():
+        own_kv().wait_recv()
+
+    heads = width // kv_width
+    shape = (heads * tokens, everything)
+    allowed = lax.broadcasted_iota(jnp.int32, shape, 1) <= (
+        lax.rem(lax.broadcasted_iota(jnp.int32, shape, 0), tokens) + place * tokens
+    )
+
+    def head_group(g):
+        def lane(h):
+            return pl.ds(pl.multiple_of((g * heads + h) * HEAD_WIDTH, HEAD_WIDTH), HEAD_WIDTH)
+
+        query = jnp.concatenate([queries[:, lane(h)] for h in range(heads)], axis=0)
+        key_rows = kv[:, pl.ds(pl.multiple_of(g * HEAD_WIDTH, HEAD_WIDTH), HEAD_WIDTH)]
+        value_rows = kv[:, pl.ds(pl.multiple_of(kv_width + g * HEAD_WIDTH, HEAD_WIDTH), HEAD_WIDTH)]
+        scores = lax.dot_general(query, key_rows, (((1,), (1,)), ((), ())), preferred_element_type=f32)
+        scores = jnp.where(allowed, scores * HEAD_WIDTH ** (-0.5), -jnp.inf)
+        raised = jnp.exp(scores - jnp.max(scores, axis=-1, keepdims=True))
+        scale = 1.0 / jnp.sum(raised, axis=-1, keepdims=True)
+        weighted = jnp.dot((raised * scale).astype(bf16), value_rows, preferred_element_type=f32).astype(bf16)
+        for h in range(heads):
+            attended[:, lane(h)] = weighted[h * tokens : (h + 1) * tokens]
+
+    loop(0, kv_width // HEAD_WIDTH, head_group)
+    load.wait()
+
+    def project(n):
+        cols = pl.ds(pl.multiple_of(n * 256, 128), 256)
+        hidden[:, cols] = jnp.dot(attended[...], weight[:, cols], preferred_element_type=f32)
+
+    loop(0, width // 256, project)
+    power = jnp.mean(hidden[...] * hidden[...], axis=-1, keepdims=True)
+    normed[...] = (hidden[...] * lax.rsqrt(power + 1e-06) * gain[...]).astype(bf16)
+
+    loop(1, line - z, lambda k: line_kv(k).wait_send())
+    loop(1, z + 1, lambda k: mate_kv(k).wait_send())
+    loop(1, line, lambda k: line_route(k).wait_send())
+
+    @pl.when(core == 0)
+    def _():
+        own_kv().wait_send()
+
+
+def attention(queries, keys, values, ids, weights, gain, out_weight, line, plane, experts_all):
+    tokens, width = queries.shape
+    kv_width = keys.shape[1]
+    capacity = tokens * ids.shape[1] * 9 // (8 * experts_all)
     slots = -(-line * capacity // 16) * 16
-    both = jnp.concatenate([route_ids[0].astype(jnp.float32), route_weights[0]], axis=1)
-    both = lax.all_gather(both, "seq", axis=0).reshape(line, CORES, tokens, 2 * top)
-    both = lax.dynamic_index_in_dim(both, core, 1, keepdims=False)
-    ids, weights = both[..., :top].astype(jnp.int32), both[..., top:]
-    members = jnp.arange(plane, dtype=jnp.int32)
-    here = members // CORES * n_seq + z * CORES + members % CORES
-    match = ids[..., None] == here
-    named = jnp.any(match, axis=2)
-    weight = jnp.sum(jnp.where(match, weights[..., None], 0.0), axis=2)
-    order = jnp.arange(tokens)
-    before = (order[None, :] < order[:, None]).astype(jnp.bfloat16)
-    slot = jnp.einsum("ts,lsp->ltp", before, named.astype(jnp.bfloat16), preferred_element_type=jnp.float32)
-    first = jnp.arange(line, dtype=jnp.int32)[:, None, None] * capacity
-    target = jnp.where(named, slot.astype(jnp.int32) + first, -1).reshape(line * tokens, plane)
-    weight = weight.reshape(line * tokens, plane)
-    at = jnp.arange(slots, dtype=jnp.int32)
-    sel = (target.T[:, None, :] == at[None, :, None]).astype(jnp.bfloat16)
-    share = jnp.where(target[:, :, None] == at, weight[:, :, None], 0.0).astype(jnp.bfloat16)
-    return sel.reshape(plane * slots, line * tokens), share.reshape(line * tokens, plane * slots)
-
-
-def attention(queries, keys, values):
-    token_rows = queries.shape[1]
-    kv_heads = keys.shape[2] // HEAD_WIDTH
-    heads_per_group = queries.shape[2] // keys.shape[2]
-    whole_keys, whole_values = (
-        lax.all_gather(keys, "seq", axis=1, tiled=True),
-        lax.all_gather(values, "seq", axis=1, tiled=True),
-    )
-    token_length = whole_keys.shape[1]
-    first_row = lax.axis_index("seq") * token_rows
-    row_index = first_row + jnp.arange(token_rows, dtype=jnp.int32)[:, None]
-    col_index = jnp.arange(token_length, dtype=jnp.int32)[None, :]
-    allowed = (col_index <= row_index)[None]
-    grouped = queries[0].reshape(token_rows, kv_heads, heads_per_group, HEAD_WIDTH)
-    results = []
-    for kv_index in range(kv_heads):
-        window = slice(kv_index * HEAD_WIDTH, (kv_index + 1) * HEAD_WIDTH)
-        scores = jnp.einsum(
-            "tgd,kd->gtk",
-            grouped[:, kv_index],
-            whole_keys[0, :, window],
-            preferred_element_type=jnp.float32,
-        ) * HEAD_WIDTH ** (-0.5)
-        scores = jnp.where(allowed, scores, -jnp.inf)
-        weighted = jnp.einsum(
-            "gtk,kd->tgd",
-            normalize_rows(scores),
-            whole_values[0, :, window],
-            preferred_element_type=jnp.float32,
-        ).astype(jnp.bfloat16)
-        results.append(weighted.reshape(token_rows, heads_per_group * HEAD_WIDTH))
-    return jnp.concatenate(results, axis=1)
+    padded = -(-experts_all // 128) * 128
+    everything = line * CORES * tokens
+    bf16, f32 = jnp.bfloat16, jnp.float32
+    vmem = pl.BlockSpec(memory_space=pltpu.VMEM)
+    dma = pltpu.SemaphoreType.DMA
+    steps = dma((line - 1,))
+    return pl.pallas_call(
+        functools.partial(attention_kernel, line, plane, capacity),
+        out_shape=(
+            jax.ShapeDtypeStruct((tokens, width), f32),
+            jax.ShapeDtypeStruct((tokens, width), bf16),
+            jax.ShapeDtypeStruct((plane * slots, line * tokens), bf16),
+            jax.ShapeDtypeStruct((line * tokens, plane * slots), bf16),
+        ),
+        in_specs=[vmem] * 6 + [pl.BlockSpec(memory_space=pl.ANY)],
+        out_specs=(vmem,) * 4,
+        scratch_shapes=[
+            pltpu.VMEM((everything, 2 * kv_width), bf16),
+            pltpu.VMEM((line, tokens, 2 * padded), bf16),
+            pltpu.VMEM((tokens, width), bf16),
+            pltpu.VMEM((width, width), bf16),
+            steps, steps, steps, steps, dma((2,)), steps, steps, dma,
+        ],
+        compiler_params=pltpu.CompilerParams(
+            collective_id=1, has_side_effects=True, vmem_limit_bytes=56 * 2**20
+        ),
+        cost_estimate=pl.CostEstimate(
+            flops=2 * tokens * width * (width + 2 * everything),
+            bytes_accessed=2 * width * width,
+            transcendentals=tokens * everything * width // HEAD_WIDTH,
+        ),
+    )(queries, keys, values, ids, weights, gain, out_weight)
 
 
 def on_device(
@@ -288,11 +427,10 @@
 ):
     n_grp, n_seq = lax.axis_size("grp"), lax.axis_size("seq")
     line, plane = n_seq // CORES, n_grp * CORES
-    sel, share = routing(route_ids, route_weights, line, plane, n_grp * n_seq)
-    attended = attention(queries, keys, values)
-    hidden_state = jnp.dot(attended, out_weight, preferred_element_type=jnp.float32)
-    power = jnp.mean(hidden_state * hidden_state, axis=-1, keepdims=True)
-    normed = (hidden_state * lax.rsqrt(power + 1e-06) * norm_gain).astype(jnp.bfloat16)
+    hidden_state, normed, sel, share = attention(
+        queries[0], keys[0], values[0], route_ids[0], route_weights[0], norm_gain[None], out_weight,
+        line, plane, n_grp * n_seq,
+    )
     return experts(normed, hidden_state, sel, share, gate_up, down_weight, line, plane)[None]
 
 

time: 226 us -> 194 us (0.86); the launches traced: 223 us -> 194 us
  Pallas kernels: 143 us -> 189 us
  waiting for transfers between devices: 17.4 us -> 0 us
  blocking collectives: 15.6 us -> 0 us
  matrix products: 14.5 us -> 0 us
  between operations: 13.6 us -> 0.02 us
  other arithmetic: 6.72 us -> 0 us
  local copies, waits for them, and re-layouts: 11.2 us -> 4.7 us
    pallas_call x0 -> x1, Pallas kernels: none -> 29.4 us  [attention(): pl.pallas_call(functools.partial(attention_kernel, line, plane, capacity)...]
    all_gather x2 -> x0, waiting for transfers between devices: 16.7 us -> none  [the longest x1 16.7 us: attention(): lax.all_gather(values, 'seq', axis=1, tiled=True)]
    pallas_call x1, Pallas kernels: 143 us -> 160 us  [experts(): pl.pallas_call(functools.partial(expert_kernel, line, plane), out_shape=j...]
    all_gather x1 -> x0, blocking collectives: 15.6 us -> none  [routing(): lax.all_gather(both, 'seq', axis=0).reshape(line, CORES, tokens, 2 * top)]
    dot_general x6 -> x0, matrix products: 10.1 us -> none  [the longest x4 5.29 us: attention(): jnp.einsum('gtk,kd->tgd', normalize_rows(scores), whole_values[0, :, wind...]
    convert_element_type x4 -> x0, other arithmetic: 5.08 us -> none  [the longest x1 1.98 us: routing(): sel = (target.T[:, None, :] == at[None, :, None]).astype(jnp.bfloat16)]
    sub x4 -> x0, matrix products: 4.33 us -> none  [normalize_rows(): raised = jnp.exp(scores - highest)]
    eq x4 -> x0, local copies, waits for them, and re-layouts: 3.89 us -> none  [the longest x2 3.8 us: routing(): target[:, :, None] == at]
  transfers between devices with their start and end apart: 2 -> 0, of which waited for: 1 -> 0; matrix products, arithmetic and copies ran while one was open for 9% -> 0% of each run, Pallas kernels for 0% -> 0%
where the time goes in v2:
time: 194 us
  Pallas kernels  189 us (97%)
  local copies, waits for them, and re-layouts  4.7 us (2%)
    pallas_call x1, Pallas kernels, experts(): pl.pallas_call(functools.partial(expert_kernel, line, plane), out_shape=j...  160 us
    pallas_call x1, Pallas kernels, attention(): pl.pallas_call(functools.partial(attention_kernel, line, plane, capacity)...  29.4 us
    unnamed x3, local copies, waits for them, and re-layouts  4.7 us

profile of v2, /device:TPU:0, one launch (start us, length us, event | category | flops | bytes accessed | tf_op | source)
XLA Modules:
  0.0 194.1 jit_solution(16335838440217059314)
XLA Ops:
  0.0 1.4 copy.10
  1.4 1.4 copy.11
  2.8 29.4 %shard_map.91 = (f32[128,2048]{1,0:T(8,128)}, bf16[128,2048]{1,0:T(8,128)(2,1)}, bf16[1152,512]{1,0:T(8,128)(2,1)}, bf16[512,1152]{1,0:T(8,128)(2,1)}) custom-call(bf16[128,2048]{1,0:T(8,128)(2,1)} %bitcast.8, bf16[128,512]{1,0:T(8,128)(2,1)} %bitcast.11, bf16[128,512]{1,0:T(8,128)(2,1)} %bitcast.12, s32[128,8]{1,0:T(8,128)} %bitcast.9, f32[128,8]{1,0:T(8,128)} %bitcast.10, ...), custom_call_target="tpu_custom_call" | custom-call | flops 2147483648 | bytes 8388608 | tf_op jit(solution)/shard_map/pallas_call | solution.py:397
  32.2 160.0 %shard_map.92 = bf16[128,2048]{1,0:T(8,128)(2,1)} custom-call(bf16[128,2048]{1,0:T(8,128)(2,1)} %get-tuple-element.9.normed, f32[128,2048]{1,0:T(8,128)} %get-tuple-element.10.hidden, bf16[1152,512]{1,0:T(8,128)(2,1)} %get-tuple-element.11.sel, bf16[512,1152]{1,0:T(8,128)(2,1)} %get-tuple-element.12.share, bf16[1,2048,1536]{2,1,0:T(8,128)(2,1)} %gate_hbm.1, ...), custom_call_target="tpu_custom_call" | custom-call | flops 10871635968 | bytes 9437184 | tf_op jit(solution)/shard_map/pallas_call | solution.py:190
  192.2 1.9 copy.13

commit v3 on v2

--- a/solution.py
+++ b/solution.py
@@ -125,11 +125,13 @@
 
         loop(0, 2 * half // 256, one)
 
-    pack(0)
-    for c in range(1, parts):
+    ahead = min(2, parts)
+    for c in range(ahead):
         pack(c)
-        first(c - 1)
-    first(parts - 1)
+    for c in range(parts):
+        if c + ahead < parts:
+            pack(c + ahead)
+        first(c)
 
     def activate(i):
         g = both[block(i), :half]

time: 194 us -> 194 us (level)
  no operation moved by 1% of the time
where the time goes in v3:
time: 194 us
  Pallas kernels  189 us (97%)
  local copies, waits for them, and re-layouts  4.7 us (2%)
    pallas_call x1, Pallas kernels, experts(): pl.pallas_call(functools.partial(expert_kernel, line, plane), out_shape=j...  160 us
    pallas_call x1, Pallas kernels, attention(): pl.pallas_call(functools.partial(attention_kernel, line, plane, capacity)...  29.4 us
    unnamed x3, local copies, waits for them, and re-layouts  4.7 us

profile of v3, /device:TPU:0, one launch (start us, length us, event | category | flops | bytes accessed | tf_op | source)
XLA Modules:
  0.0 194.1 jit_solution(12396996926477236510)
XLA Ops:
  0.0 1.4 copy.10
  1.4 1.4 copy.11
  2.8 29.4 %shard_map.91 = (f32[128,2048]{1,0:T(8,128)}, bf16[128,2048]{1,0:T(8,128)(2,1)}, bf16[1152,512]{1,0:T(8,128)(2,1)}, bf16[512,1152]{1,0:T(8,128)(2,1)}) custom-call(bf16[128,2048]{1,0:T(8,128)(2,1)} %bitcast.8, bf16[128,512]{1,0:T(8,128)(2,1)} %bitcast.11, bf16[128,512]{1,0:T(8,128)(2,1)} %bitcast.12, s32[128,8]{1,0:T(8,128)} %bitcast.9, f32[128,8]{1,0:T(8,128)} %bitcast.10, ...), custom_call_target="tpu_custom_call" | custom-call | flops 2147483648 | bytes 8388608 | tf_op jit(solution)/shard_map/pallas_call | solution.py:399
  32.2 160.0 %shard_map.92 = bf16[128,2048]{1,0:T(8,128)(2,1)} custom-call(bf16[128,2048]{1,0:T(8,128)(2,1)} %get-tuple-element.9.normed, f32[128,2048]{1,0:T(8,128)} %get-tuple-element.10.hidden, bf16[1152,512]{1,0:T(8,128)(2,1)} %get-tuple-element.11.sel, bf16[512,1152]{1,0:T(8,128)(2,1)} %get-tuple-element.12.share, bf16[1,2048,1536]{2,1,0:T(8,128)(2,1)} %gate_hbm.1, ...), custom_call_target="tpu_custom_call" | custom-call | flops 10871635968 | bytes 9437184 | tf_op jit(solution)/shard_map/pallas_call | solution.py:192
  192.2 1.9 copy.13
